TPU v7x, 32 devices: a whole 2x2x4 slice. The times are simulated.
32 devices in a mesh: blk: 16 (over z, y, core), grp: 2 (over x).
Axes of the slice: x: 2, y: 2, z: 4, core: 2. Of those that a mesh axis runs over, the one named last changes fastest.
Arguments:
- orbitals: float32 [8192, 512], P('blk'), may hold values from -6 to 6
- points: float32 [3, 8192], P(None, 'blk'), may hold values from 0 to 1
Outputs:
- exchange_vectors: float32 [8192, 512], P('blk')
All inputs are finite; a program needn't handle non-finite values.
Results may differ from a plain program's by a relative error of at most 0.0003.
Values sent between devices are 32-bit elements; how exact they have to be, the bound alone decides.
A program may use at most 64 MiB of HBM per device.

v0:
```python
import jax
import jax.numpy as jnp
from jax import lax
from jax.sharding import PartitionSpec as P


def shifted(block, axis, distance):
    devices = range(lax.axis_size(axis))
    route = [((i - distance) % len(devices), i) for i in devices]
    return lax.ppermute(block, axis, route)


def kernel(near_coords, far_coords):
    squared = jnp.zeros((near_coords.shape[1], far_coords.shape[1]), jnp.float32)
    for axis_index in range(3):
        spacing = near_coords[axis_index][:, None] - far_coords[axis_index][None, :]
        squared = squared + spacing * spacing
    return lax.rsqrt(squared + 0.0025)


def shards(orbitals, points):
    highest = lax.Precision.HIGHEST
    row_count = orbitals.shape[0]
    block_count = lax.axis_size("blk")
    group_count = lax.axis_size("grp")
    weight = 1.0 / (row_count * block_count)
    group_index = lax.axis_index("grp")

    def tile(applied, far_piece):
        far_rows, far_coords = far_piece
        gram_tile = lax.dot_general(orbitals, far_rows, (((1,), (1,)), ((), ())), precision=highest)
        screened = gram_tile * kernel(points, far_coords)
        return applied - weight * jnp.dot(screened, far_rows, precision=highest)

    slice_size = row_count // group_count
    slice_start = group_index * slice_size
    far_rows = lax.dynamic_slice_in_dim(orbitals, slice_start, slice_size, 0)
    far_coords = lax.dynamic_slice_in_dim(points, slice_start, slice_size, 1)
    carried = (far_rows, far_coords)
    applied = tile(jnp.zeros(orbitals.shape, jnp.float32), carried)

    def advance_rows(cycle_turn, loop_state):
        piece_now, applied_now = loop_state
        piece_next = shifted((piece_now[0], piece_now[1]), "blk", -1)
        return (piece_next, tile(applied_now, piece_next))

    carried, applied = lax.fori_loop(0, block_count - 1, advance_rows, (carried, applied))
    applied = lax.psum(applied, "grp")
    partial_correlation = weight * jnp.dot(orbitals.T, applied, precision=highest)
    correlation = lax.psum(partial_correlation, "blk")
    factor = jnp.linalg.cholesky(-correlation)
    return lax.linalg.triangular_solve(
        factor, applied, left_side=False, lower=True, transpose_a=True
    )


def solution(mesh):
    return jax.shard_map(
        shards,
        mesh=mesh,
        in_specs=(P("blk", None), P(None, "blk")),
        out_specs=P("blk", None),
        check_vma=False,
    )
```

profile of v0, /device:TPU:1, one launch (start us, length us, event | category | flops | bytes accessed | tf_op | source)
XLA Modules:
  0.0 504.6 jit_solution(552813081495643585)
XLA Ops:
  11.4 200.9 %while.15 = (s32[]{:T(128)}, f32[256,512]{1,0:T(8,128)S(1)}, f32[3,256]{1,0:T(4,128)S(1)}, f32[512,512]{1,0:T(8,128)S(1)}, f32[512,512]{1,0:T(8,128)S(1)}, /*index=5*/f32[3,512]{1,0:T(4,128)S(1)}, s32[]{:T(128)}) while((s32[]{:T(128)}, f32[256,512]{1,0:T(8,128)S(1)}, f32[3,256]{1,0:T(4,128)S(1)}, f32[512,512]{1,0:T(8,128)S(1)}, ...), condition=%wide.region_1.0_spmd, body=%wide.region_0.0_spmd.sunk | while | flops 1612447744 | bytes 8434845 | solution.py:47
  11.5 5.4 %collective-permute-start.1 = (f32[3,256]{1,0:T(4,128)S(1)}, f32[3,256]{1,0:T(4,128)S(1)}, u32[]{:S(2)}, u32[]{:S(2)}) collective-permute-start(f32[3,256]{1,0:T(4,128)S(1)} %get-tuple-element.181), channel_id=1, source_target_pairs={{2,0},{4,2},{6,4},{8,6},{10,8},{12,10},{14,12},{16,14},{18,16},{20... | collective-permute-start | bytes 9224 | tf_op jit(solution)/shard_map/while/body/eval_jaxpr/ppermute | solution.py:10
  17.0 4.0 collective-permute-done.1
  22.1 1.2 fusion.67
  23.3 2.8 collective-permute-start
  26.1 4.6 collective-permute-start.1
  30.7 1.3 collective-permute-done.1
  33.1 1.2 fusion.67
  34.4 5.5 %collective-permute-start = (f32[256,512]{1,0:T(8,128)S(1)}, f32[256,512]{1,0:T(8,128)S(1)}, u32[]{:S(2)}, u32[]{:S(2)}) collective-permute-start(f32[256,512]{1,0:T(8,128)S(1)} %get-tuple-element.180), channel_id=1, source_target_pairs={{2,0},{4,2},{6,4},{8,6},{10,8},{12,10},{14,12},{16,14},{18,16},{20... | collective-permute-start | bytes 1572872 | tf_op jit(solution)/shard_map/while/body/eval_jaxpr/ppermute | solution.py:10
  39.8 4.6 collective-permute-start.1
  46.3 1.2 fusion.67
  47.6 6.0 %collective-permute-start = (f32[256,512]{1,0:T(8,128)S(1)}, f32[256,512]{1,0:T(8,128)S(1)}, u32[]{:S(2)}, u32[]{:S(2)}) collective-permute-start(f32[256,512]{1,0:T(8,128)S(1)} %get-tuple-element.180), channel_id=1, source_target_pairs={{2,0},{4,2},{6,4},{8,6},{10,8},{12,10},{14,12},{16,14},{18,16},{20... | collective-permute-start | bytes 1572872 | tf_op jit(solution)/shard_map/while/body/eval_jaxpr/ppermute | solution.py:10
  53.5 4.6 collective-permute-start.1
  60.1 1.2 fusion.67
  61.3 6.0 %collective-permute-start = (f32[256,512]{1,0:T(8,128)S(1)}, f32[256,512]{1,0:T(8,128)S(1)}, u32[]{:S(2)}, u32[]{:S(2)}) collective-permute-start(f32[256,512]{1,0:T(8,128)S(1)} %get-tuple-element.180), channel_id=1, source_target_pairs={{2,0},{4,2},{6,4},{8,6},{10,8},{12,10},{14,12},{16,14},{18,16},{20... | collective-permute-start | bytes 1572872 | tf_op jit(solution)/shard_map/while/body/eval_jaxpr/ppermute | solution.py:10
  67.3 4.6 collective-permute-start.1
  73.8 1.2 fusion.67
  75.0 6.0 %collective-permute-start = (f32[256,512]{1,0:T(8,128)S(1)}, f32[256,512]{1,0:T(8,128)S(1)}, u32[]{:S(2)}, u32[]{:S(2)}) collective-permute-start(f32[256,512]{1,0:T(8,128)S(1)} %get-tuple-element.180), channel_id=1, source_target_pairs={{2,0},{4,2},{6,4},{8,6},{10,8},{12,10},{14,12},{16,14},{18,16},{20... | collective-permute-start | bytes 1572872 | tf_op jit(solution)/shard_map/while/body/eval_jaxpr/ppermute | solution.py:10
  81.0 4.6 collective-permute-start.1
  87.5 1.2 fusion.67
  88.7 6.0 %collective-permute-start = (f32[256,512]{1,0:T(8,128)S(1)}, f32[256,512]{1,0:T(8,128)S(1)}, u32[]{:S(2)}, u32[]{:S(2)}) collective-permute-start(f32[256,512]{1,0:T(8,128)S(1)} %get-tuple-element.180), channel_id=1, source_target_pairs={{2,0},{4,2},{6,4},{8,6},{10,8},{12,10},{14,12},{16,14},{18,16},{20... | collective-permute-start | bytes 1572872 | tf_op jit(solution)/shard_map/while/body/eval_jaxpr/ppermute | solution.py:10
  94.7 4.6 collective-permute-start.1
  101.2 1.2 fusion.67
  102.5 6.0 %collective-permute-start = (f32[256,512]{1,0:T(8,128)S(1)}, f32[256,512]{1,0:T(8,128)S(1)}, u32[]{:S(2)}, u32[]{:S(2)}) collective-permute-start(f32[256,512]{1,0:T(8,128)S(1)} %get-tuple-element.180), channel_id=1, source_target_pairs={{2,0},{4,2},{6,4},{8,6},{10,8},{12,10},{14,12},{16,14},{18,16},{20... | collective-permute-start | bytes 1572872 | tf_op jit(solution)/shard_map/while/body/eval_jaxpr/ppermute | solution.py:10
  108.5 4.6 collective-permute-start.1
  115.0 1.2 fusion.67
  116.2 6.0 %collective-permute-start = (f32[256,512]{1,0:T(8,128)S(1)}, f32[256,512]{1,0:T(8,128)S(1)}, u32[]{:S(2)}, u32[]{:S(2)}) collective-permute-start(f32[256,512]{1,0:T(8,128)S(1)} %get-tuple-element.180), channel_id=1, source_target_pairs={{2,0},{4,2},{6,4},{8,6},{10,8},{12,10},{14,12},{16,14},{18,16},{20... | collective-permute-start | bytes 1572872 | tf_op jit(solution)/shard_map/while/body/eval_jaxpr/ppermute | solution.py:10
  122.2 4.6 collective-permute-start.1
  128.7 1.2 fusion.67
  129.9 6.0 %collective-permute-start = (f32[256,512]{1,0:T(8,128)S(1)}, f32[256,512]{1,0:T(8,128)S(1)}, u32[]{:S(2)}, u32[]{:S(2)}) collective-permute-start(f32[256,512]{1,0:T(8,128)S(1)} %get-tuple-element.180), channel_id=1, source_target_pairs={{2,0},{4,2},{6,4},{8,6},{10,8},{12,10},{14,12},{16,14},{18,16},{20... | collective-permute-start | bytes 1572872 | tf_op jit(solution)/shard_map/while/body/eval_jaxpr/ppermute | solution.py:10
  135.9 4.6 collective-permute-start.1
  142.4 1.2 fusion.67
  143.7 6.0 %collective-permute-start = (f32[256,512]{1,0:T(8,128)S(1)}, f32[256,512]{1,0:T(8,128)S(1)}, u32[]{:S(2)}, u32[]{:S(2)}) collective-permute-start(f32[256,512]{1,0:T(8,128)S(1)} %get-tuple-element.180), channel_id=1, source_target_pairs={{2,0},{4,2},{6,4},{8,6},{10,8},{12,10},{14,12},{16,14},{18,16},{20... | collective-permute-start | bytes 1572872 | tf_op jit(solution)/shard_map/while/body/eval_jaxpr/ppermute | solution.py:10
  149.6 4.6 collective-permute-start.1
  156.1 1.2 fusion.67
  157.4 6.0 %collective-permute-start = (f32[256,512]{1,0:T(8,128)S(1)}, f32[256,512]{1,0:T(8,128)S(1)}, u32[]{:S(2)}, u32[]{:S(2)}) collective-permute-start(f32[256,512]{1,0:T(8,128)S(1)} %get-tuple-element.180), channel_id=1, source_target_pairs={{2,0},{4,2},{6,4},{8,6},{10,8},{12,10},{14,12},{16,14},{18,16},{20... | collective-permute-start | bytes 1572872 | tf_op jit(solution)/shard_map/while/body/eval_jaxpr/ppermute | solution.py:10
  163.4 4.6 collective-permute-start.1
  171.1 6.0 %collective-permute-start = (f32[256,512]{1,0:T(8,128)S(1)}, f32[256,512]{1,0:T(8,128)S(1)}, u32[]{:S(2)}, u32[]{:S(2)}) collective-permute-start(f32[256,512]{1,0:T(8,128)S(1)} %get-tuple-element.180), channel_id=1, source_target_pairs={{2,0},{4,2},{6,4},{8,6},{10,8},{12,10},{14,12},{16,14},{18,16},{20... | collective-permute-start | bytes 1572872 | tf_op jit(solution)/shard_map/while/body/eval_jaxpr/ppermute | solution.py:10
  177.1 4.6 collective-permute-start.1
  184.8 6.0 %collective-permute-start = (f32[256,512]{1,0:T(8,128)S(1)}, f32[256,512]{1,0:T(8,128)S(1)}, u32[]{:S(2)}, u32[]{:S(2)}) collective-permute-start(f32[256,512]{1,0:T(8,128)S(1)} %get-tuple-element.180), channel_id=1, source_target_pairs={{2,0},{4,2},{6,4},{8,6},{10,8},{12,10},{14,12},{16,14},{18,16},{20... | collective-permute-start | bytes 1572872 | tf_op jit(solution)/shard_map/while/body/eval_jaxpr/ppermute | solution.py:10
  190.8 4.6 collective-permute-start.1
  197.3 1.2 fusion.67
  198.6 6.0 %collective-permute-start = (f32[256,512]{1,0:T(8,128)S(1)}, f32[256,512]{1,0:T(8,128)S(1)}, u32[]{:S(2)}, u32[]{:S(2)}) collective-permute-start(f32[256,512]{1,0:T(8,128)S(1)} %get-tuple-element.180), channel_id=1, source_target_pairs={{2,0},{4,2},{6,4},{8,6},{10,8},{12,10},{14,12},{16,14},{18,16},{20... | collective-permute-start | bytes 1572872 | tf_op jit(solution)/shard_map/while/body/eval_jaxpr/ppermute | solution.py:10
  204.5 4.6 collective-permute-start.1
  211.0 1.2 fusion.67
  213.5 46.6 %all-reduce.4.cloned.1.call-done = f32[512,512]{1,0:T(8,128)} async-done(((f32[512,512]{1,0:T(8,128)}), f32[512,512]{1,0:T(8,128)}) %all-reduce.4.cloned.1.call-update) | async-done | bytes 1048592 | tf_op jit(solution)/shard_map/psum | solution.py:48
  260.1 4.0 fusion.1
  264.1 92.7 %all-reduce.6.cloned.1.call-done = f32[512,512]{0,1:T(8,128)} async-done(((f32[512,512]{0,1:T(8,128)}), f32[512,512]{0,1:T(8,128)}) %all-reduce.6.cloned.1.call-update) | async-done | bytes 1048592 | tf_op jit(solution)/shard_map/psum | solution.py:50
  356.8 1.3 neg.3
  359.6 11.7 %cholesky.103 = f32[128,128]{1,0:T(8,128)S(1)} custom-call(f32[128,128]{1,0:T(8,128)S(1)} %cholesky.263), custom_call_target="Cholesky" | custom-call | tf_op jit(solution)/shard_map/jit(cholesky)/cholesky | solution.py:51
  371.5 9.8 %custom-call.30 = f32[1,128,128]{1,2,0:T(8,128)S(1)} custom-call(f32[1,128,128]{2,1,0:T(8,128)S(1)} %get-tuple-element.83), custom_call_target="InvertDiagBlocksLowerTriangular" | custom-call | tf_op jit(solution)/shard_map/jit(cholesky)/cholesky | solution.py:51
  382.0 11.9 %cholesky.215 = f32[128,128]{1,0:T(8,128)S(1)} custom-call(f32[128,128]{1,0:T(8,128)S(1)} %cholesky.267), custom_call_target="Cholesky" | custom-call | tf_op jit(solution)/shard_map/jit(cholesky)/cholesky | solution.py:51
  394.0 9.8 %custom-call.31 = f32[1,128,128]{1,2,0:T(8,128)S(1)} custom-call(f32[1,128,128]{2,1,0:T(8,128)S(1)} %get-tuple-element.80), custom_call_target="InvertDiagBlocksLowerTriangular" | custom-call | tf_op jit(solution)/shard_map/jit(cholesky)/cholesky | solution.py:51
  404.4 11.7 %cholesky.236 = f32[128,128]{1,0:T(8,128)S(1)} custom-call(f32[128,128]{1,0:T(8,128)S(1)} %cholesky.272), custom_call_target="Cholesky" | custom-call | tf_op jit(solution)/shard_map/jit(cholesky)/cholesky | solution.py:51
  416.9 9.8 %custom-call.32 = f32[1,128,128]{1,2,0:T(8,128)S(1)} custom-call(f32[1,128,128]{2,1,0:T(8,128)S(1)} %get-tuple-element.77), custom_call_target="InvertDiagBlocksLowerTriangular" | custom-call | tf_op jit(solution)/shard_map/jit(cholesky)/cholesky | solution.py:51
  427.3 11.9 %cholesky.253 = f32[128,128]{1,0:T(8,128)S(1)} custom-call(f32[128,128]{1,0:T(8,128)S(1)} %convolution_subtract_fusion.5), custom_call_target="Cholesky" | custom-call | tf_op jit(solution)/shard_map/jit(cholesky)/cholesky | solution.py:51
  443.3 8.5 %while.16 = (s32[]{:T(128)}, f32[512,512]{1,0:T(8,128)S(1)}, s32[4,2]{0,1:T(2,128)S(1)}, f32[4,128,128]{2,1,0:T(8,128)S(1)}, s32[]{:T(128)}) while((s32[]{:T(128)}, f32[512,512]{1,0:T(8,128)S(1)}, s32[4,2]{0,1:T(2,128)S(1)}, f32[4,128,128]{2,1,0:T(8,128)S(1)}, s32[]{:T(128)}) %tuple.55), condition=%wide.while_cond, body=%wide.while_body.sunk | while | flops 2 | bytes 131181 | solution.py:52
  444.0 1.4 bitcast_dynamic-update-slice_fusion.2
  446.1 1.4 bitcast_dynamic-update-slice_fusion.2
  448.2 1.4 bitcast_dynamic-update-slice_fusion.2
  450.3 1.4 bitcast_dynamic-update-slice_fusion.2
  451.8 39.3 %custom-call.33 = f32[4,128,128]{1,2,0:T(8,128)S(1)} custom-call(f32[4,128,128]{2,1,0:T(8,128)S(1)} %get-tuple-element.45), custom_call_target="InvertDiagBlocksLowerTriangular" | custom-call | tf_op jit(solution)/shard_map/triangular_solve | solution.py:52
  494.0 1.5 convolution_subtract_fusion.2
  496.0 1.3 copy.4
  (164 shorter events, 47.1 us)
Async XLA Ops:
  6.5 2.7 copy-start.3
  6.5 253.5 %all-reduce.4.cloned.1.call-start = ((), (), s32[]{:S(2)}) async-start(), calls=%async_computation | async-start | bytes 2097152 | tf_op jit(solution)/shard_map/psum | solution.py:48
  8.1 1.1 copy-start.4
  11.4 9.6 %collective-permute-start = (f32[256,512]{1,0:T(8,128)S(1)}, f32[256,512]{1,0:T(8,128)S(1)}, u32[]{:S(2)}, u32[]{:S(2)}) collective-permute-start(f32[256,512]{1,0:T(8,128)S(1)} %get-tuple-element.180), channel_id=1, source_target_pairs={{2,0},{4,2},{6,4},{8,6},{10,8},{12,10},{14,12},{16,14},{18,16},{20... | collective-permute-start | bytes 1572872 | tf_op jit(solution)/shard_map/while/body/eval_jaxpr/ppermute | solution.py:10
  11.5 9.5 %collective-permute-start.1 = (f32[3,256]{1,0:T(4,128)S(1)}, f32[3,256]{1,0:T(4,128)S(1)}, u32[]{:S(2)}, u32[]{:S(2)}) collective-permute-start(f32[3,256]{1,0:T(4,128)S(1)} %get-tuple-element.181), channel_id=1, source_target_pairs={{2,0},{4,2},{6,4},{8,6},{10,8},{12,10},{14,12},{16,14},{18,16},{20... | collective-permute-start | bytes 9224 | tf_op jit(solution)/shard_map/while/body/eval_jaxpr/ppermute | solution.py:10
  23.3 8.7 %collective-permute-start = (f32[256,512]{1,0:T(8,128)S(1)}, f32[256,512]{1,0:T(8,128)S(1)}, u32[]{:S(2)}, u32[]{:S(2)}) collective-permute-start(f32[256,512]{1,0:T(8,128)S(1)} %get-tuple-element.180), channel_id=1, source_target_pairs={{2,0},{4,2},{6,4},{8,6},{10,8},{12,10},{14,12},{16,14},{18,16},{20... | collective-permute-start | bytes 1572872 | tf_op jit(solution)/shard_map/while/body/eval_jaxpr/ppermute | solution.py:10
  26.1 6.0 %collective-permute-start.1 = (f32[3,256]{1,0:T(4,128)S(1)}, f32[3,256]{1,0:T(4,128)S(1)}, u32[]{:S(2)}, u32[]{:S(2)}) collective-permute-start(f32[3,256]{1,0:T(4,128)S(1)} %get-tuple-element.181), channel_id=1, source_target_pairs={{2,0},{4,2},{6,4},{8,6},{10,8},{12,10},{14,12},{16,14},{18,16},{20... | collective-permute-start | bytes 9224 | tf_op jit(solution)/shard_map/while/body/eval_jaxpr/ppermute | solution.py:10
  34.4 10.9 %collective-permute-start = (f32[256,512]{1,0:T(8,128)S(1)}, f32[256,512]{1,0:T(8,128)S(1)}, u32[]{:S(2)}, u32[]{:S(2)}) collective-permute-start(f32[256,512]{1,0:T(8,128)S(1)} %get-tuple-element.180), channel_id=1, source_target_pairs={{2,0},{4,2},{6,4},{8,6},{10,8},{12,10},{14,12},{16,14},{18,16},{20... | collective-permute-start | bytes 1572872 | tf_op jit(solution)/shard_map/while/body/eval_jaxpr/ppermute | solution.py:10
  39.8 5.4 %collective-permute-start.1 = (f32[3,256]{1,0:T(4,128)S(1)}, f32[3,256]{1,0:T(4,128)S(1)}, u32[]{:S(2)}, u32[]{:S(2)}) collective-permute-start(f32[3,256]{1,0:T(4,128)S(1)} %get-tuple-element.181), channel_id=1, source_target_pairs={{2,0},{4,2},{6,4},{8,6},{10,8},{12,10},{14,12},{16,14},{18,16},{20... | collective-permute-start | bytes 9224 | tf_op jit(solution)/shard_map/while/body/eval_jaxpr/ppermute | solution.py:10
  47.6 11.4 %collective-permute-start = (f32[256,512]{1,0:T(8,128)S(1)}, f32[256,512]{1,0:T(8,128)S(1)}, u32[]{:S(2)}, u32[]{:S(2)}) collective-permute-start(f32[256,512]{1,0:T(8,128)S(1)} %get-tuple-element.180), channel_id=1, source_target_pairs={{2,0},{4,2},{6,4},{8,6},{10,8},{12,10},{14,12},{16,14},{18,16},{20... | collective-permute-start | bytes 1572872 | tf_op jit(solution)/shard_map/while/body/eval_jaxpr/ppermute | solution.py:10
  53.5 5.4 %collective-permute-start.1 = (f32[3,256]{1,0:T(4,128)S(1)}, f32[3,256]{1,0:T(4,128)S(1)}, u32[]{:S(2)}, u32[]{:S(2)}) collective-permute-start(f32[3,256]{1,0:T(4,128)S(1)} %get-tuple-element.181), channel_id=1, source_target_pairs={{2,0},{4,2},{6,4},{8,6},{10,8},{12,10},{14,12},{16,14},{18,16},{20... | collective-permute-start | bytes 9224 | tf_op jit(solution)/shard_map/while/body/eval_jaxpr/ppermute | solution.py:10
  61.3 11.4 %collective-permute-start = (f32[256,512]{1,0:T(8,128)S(1)}, f32[256,512]{1,0:T(8,128)S(1)}, u32[]{:S(2)}, u32[]{:S(2)}) collective-permute-start(f32[256,512]{1,0:T(8,128)S(1)} %get-tuple-element.180), channel_id=1, source_target_pairs={{2,0},{4,2},{6,4},{8,6},{10,8},{12,10},{14,12},{16,14},{18,16},{20... | collective-permute-start | bytes 1572872 | tf_op jit(solution)/shard_map/while/body/eval_jaxpr/ppermute | solution.py:10
  67.3 5.4 %collective-permute-start.1 = (f32[3,256]{1,0:T(4,128)S(1)}, f32[3,256]{1,0:T(4,128)S(1)}, u32[]{:S(2)}, u32[]{:S(2)}) collective-permute-start(f32[3,256]{1,0:T(4,128)S(1)} %get-tuple-element.181), channel_id=1, source_target_pairs={{2,0},{4,2},{6,4},{8,6},{10,8},{12,10},{14,12},{16,14},{18,16},{20... | collective-permute-start | bytes 9224 | tf_op jit(solution)/shard_map/while/body/eval_jaxpr/ppermute | solution.py:10
  75.0 11.4 %collective-permute-start = (f32[256,512]{1,0:T(8,128)S(1)}, f32[256,512]{1,0:T(8,128)S(1)}, u32[]{:S(2)}, u32[]{:S(2)}) collective-permute-start(f32[256,512]{1,0:T(8,128)S(1)} %get-tuple-element.180), channel_id=1, source_target_pairs={{2,0},{4,2},{6,4},{8,6},{10,8},{12,10},{14,12},{16,14},{18,16},{20... | collective-permute-start | bytes 1572872 | tf_op jit(solution)/shard_map/while/body/eval_jaxpr/ppermute | solution.py:10
  81.0 5.4 %collective-permute-start.1 = (f32[3,256]{1,0:T(4,128)S(1)}, f32[3,256]{1,0:T(4,128)S(1)}, u32[]{:S(2)}, u32[]{:S(2)}) collective-permute-start(f32[3,256]{1,0:T(4,128)S(1)} %get-tuple-element.181), channel_id=1, source_target_pairs={{2,0},{4,2},{6,4},{8,6},{10,8},{12,10},{14,12},{16,14},{18,16},{20... | collective-permute-start | bytes 9224 | tf_op jit(solution)/shard_map/while/body/eval_jaxpr/ppermute | solution.py:10
  88.7 11.4 %collective-permute-start = (f32[256,512]{1,0:T(8,128)S(1)}, f32[256,512]{1,0:T(8,128)S(1)}, u32[]{:S(2)}, u32[]{:S(2)}) collective-permute-start(f32[256,512]{1,0:T(8,128)S(1)} %get-tuple-element.180), channel_id=1, source_target_pairs={{2,0},{4,2},{6,4},{8,6},{10,8},{12,10},{14,12},{16,14},{18,16},{20... | collective-permute-start | bytes 1572872 | tf_op jit(solution)/shard_map/while/body/eval_jaxpr/ppermute | solution.py:10
  94.7 5.4 %collective-permute-start.1 = (f32[3,256]{1,0:T(4,128)S(1)}, f32[3,256]{1,0:T(4,128)S(1)}, u32[]{:S(2)}, u32[]{:S(2)}) collective-permute-start(f32[3,256]{1,0:T(4,128)S(1)} %get-tuple-element.181), channel_id=1, source_target_pairs={{2,0},{4,2},{6,4},{8,6},{10,8},{12,10},{14,12},{16,14},{18,16},{20... | collective-permute-start | bytes 9224 | tf_op jit(solution)/shard_map/while/body/eval_jaxpr/ppermute | solution.py:10
  102.5 11.4 %collective-permute-start = (f32[256,512]{1,0:T(8,128)S(1)}, f32[256,512]{1,0:T(8,128)S(1)}, u32[]{:S(2)}, u32[]{:S(2)}) collective-permute-start(f32[256,512]{1,0:T(8,128)S(1)} %get-tuple-element.180), channel_id=1, source_target_pairs={{2,0},{4,2},{6,4},{8,6},{10,8},{12,10},{14,12},{16,14},{18,16},{20... | collective-permute-start | bytes 1572872 | tf_op jit(solution)/shard_map/while/body/eval_jaxpr/ppermute | solution.py:10
  108.5 5.4 %collective-permute-start.1 = (f32[3,256]{1,0:T(4,128)S(1)}, f32[3,256]{1,0:T(4,128)S(1)}, u32[]{:S(2)}, u32[]{:S(2)}) collective-permute-start(f32[3,256]{1,0:T(4,128)S(1)} %get-tuple-element.181), channel_id=1, source_target_pairs={{2,0},{4,2},{6,4},{8,6},{10,8},{12,10},{14,12},{16,14},{18,16},{20... | collective-permute-start | bytes 9224 | tf_op jit(solution)/shard_map/while/body/eval_jaxpr/ppermute | solution.py:10
  116.2 11.4 %collective-permute-start = (f32[256,512]{1,0:T(8,128)S(1)}, f32[256,512]{1,0:T(8,128)S(1)}, u32[]{:S(2)}, u32[]{:S(2)}) collective-permute-start(f32[256,512]{1,0:T(8,128)S(1)} %get-tuple-element.180), channel_id=1, source_target_pairs={{2,0},{4,2},{6,4},{8,6},{10,8},{12,10},{14,12},{16,14},{18,16},{20... | collective-permute-start | bytes 1572872 | tf_op jit(solution)/shard_map/while/body/eval_jaxpr/ppermute | solution.py:10
  122.2 5.4 %collective-permute-start.1 = (f32[3,256]{1,0:T(4,128)S(1)}, f32[3,256]{1,0:T(4,128)S(1)}, u32[]{:S(2)}, u32[]{:S(2)}) collective-permute-start(f32[3,256]{1,0:T(4,128)S(1)} %get-tuple-element.181), channel_id=1, source_target_pairs={{2,0},{4,2},{6,4},{8,6},{10,8},{12,10},{14,12},{16,14},{18,16},{20... | collective-permute-start | bytes 9224 | tf_op jit(solution)/shard_map/while/body/eval_jaxpr/ppermute | solution.py:10
  129.9 11.4 %collective-permute-start = (f32[256,512]{1,0:T(8,128)S(1)}, f32[256,512]{1,0:T(8,128)S(1)}, u32[]{:S(2)}, u32[]{:S(2)}) collective-permute-start(f32[256,512]{1,0:T(8,128)S(1)} %get-tuple-element.180), channel_id=1, source_target_pairs={{2,0},{4,2},{6,4},{8,6},{10,8},{12,10},{14,12},{16,14},{18,16},{20... | collective-permute-start | bytes 1572872 | tf_op jit(solution)/shard_map/while/body/eval_jaxpr/ppermute | solution.py:10
  135.9 5.4 %collective-permute-start.1 = (f32[3,256]{1,0:T(4,128)S(1)}, f32[3,256]{1,0:T(4,128)S(1)}, u32[]{:S(2)}, u32[]{:S(2)}) collective-permute-start(f32[3,256]{1,0:T(4,128)S(1)} %get-tuple-element.181), channel_id=1, source_target_pairs={{2,0},{4,2},{6,4},{8,6},{10,8},{12,10},{14,12},{16,14},{18,16},{20... | collective-permute-start | bytes 9224 | tf_op jit(solution)/shard_map/while/body/eval_jaxpr/ppermute | solution.py:10
  143.7 11.4 %collective-permute-start = (f32[256,512]{1,0:T(8,128)S(1)}, f32[256,512]{1,0:T(8,128)S(1)}, u32[]{:S(2)}, u32[]{:S(2)}) collective-permute-start(f32[256,512]{1,0:T(8,128)S(1)} %get-tuple-element.180), channel_id=1, source_target_pairs={{2,0},{4,2},{6,4},{8,6},{10,8},{12,10},{14,12},{16,14},{18,16},{20... | collective-permute-start | bytes 1572872 | tf_op jit(solution)/shard_map/while/body/eval_jaxpr/ppermute | solution.py:10
  149.6 5.4 %collective-permute-start.1 = (f32[3,256]{1,0:T(4,128)S(1)}, f32[3,256]{1,0:T(4,128)S(1)}, u32[]{:S(2)}, u32[]{:S(2)}) collective-permute-start(f32[3,256]{1,0:T(4,128)S(1)} %get-tuple-element.181), channel_id=1, source_target_pairs={{2,0},{4,2},{6,4},{8,6},{10,8},{12,10},{14,12},{16,14},{18,16},{20... | collective-permute-start | bytes 9224 | tf_op jit(solution)/shard_map/while/body/eval_jaxpr/ppermute | solution.py:10
  157.4 11.4 %collective-permute-start = (f32[256,512]{1,0:T(8,128)S(1)}, f32[256,512]{1,0:T(8,128)S(1)}, u32[]{:S(2)}, u32[]{:S(2)}) collective-permute-start(f32[256,512]{1,0:T(8,128)S(1)} %get-tuple-element.180), channel_id=1, source_target_pairs={{2,0},{4,2},{6,4},{8,6},{10,8},{12,10},{14,12},{16,14},{18,16},{20... | collective-permute-start | bytes 1572872 | tf_op jit(solution)/shard_map/while/body/eval_jaxpr/ppermute | solution.py:10
  163.4 5.4 %collective-permute-start.1 = (f32[3,256]{1,0:T(4,128)S(1)}, f32[3,256]{1,0:T(4,128)S(1)}, u32[]{:S(2)}, u32[]{:S(2)}) collective-permute-start(f32[3,256]{1,0:T(4,128)S(1)} %get-tuple-element.181), channel_id=1, source_target_pairs={{2,0},{4,2},{6,4},{8,6},{10,8},{12,10},{14,12},{16,14},{18,16},{20... | collective-permute-start | bytes 9224 | tf_op jit(solution)/shard_map/while/body/eval_jaxpr/ppermute | solution.py:10
  171.1 11.4 %collective-permute-start = (f32[256,512]{1,0:T(8,128)S(1)}, f32[256,512]{1,0:T(8,128)S(1)}, u32[]{:S(2)}, u32[]{:S(2)}) collective-permute-start(f32[256,512]{1,0:T(8,128)S(1)} %get-tuple-element.180), channel_id=1, source_target_pairs={{2,0},{4,2},{6,4},{8,6},{10,8},{12,10},{14,12},{16,14},{18,16},{20... | collective-permute-start | bytes 1572872 | tf_op jit(solution)/shard_map/while/body/eval_jaxpr/ppermute | solution.py:10
  177.1 5.4 %collective-permute-start.1 = (f32[3,256]{1,0:T(4,128)S(1)}, f32[3,256]{1,0:T(4,128)S(1)}, u32[]{:S(2)}, u32[]{:S(2)}) collective-permute-start(f32[3,256]{1,0:T(4,128)S(1)} %get-tuple-element.181), channel_id=1, source_target_pairs={{2,0},{4,2},{6,4},{8,6},{10,8},{12,10},{14,12},{16,14},{18,16},{20... | collective-permute-start | bytes 9224 | tf_op jit(solution)/shard_map/while/body/eval_jaxpr/ppermute | solution.py:10
  184.8 11.4 %collective-permute-start = (f32[256,512]{1,0:T(8,128)S(1)}, f32[256,512]{1,0:T(8,128)S(1)}, u32[]{:S(2)}, u32[]{:S(2)}) collective-permute-start(f32[256,512]{1,0:T(8,128)S(1)} %get-tuple-element.180), channel_id=1, source_target_pairs={{2,0},{4,2},{6,4},{8,6},{10,8},{12,10},{14,12},{16,14},{18,16},{20... | collective-permute-start | bytes 1572872 | tf_op jit(solution)/shard_map/while/body/eval_jaxpr/ppermute | solution.py:10
  190.8 5.4 %collective-permute-start.1 = (f32[3,256]{1,0:T(4,128)S(1)}, f32[3,256]{1,0:T(4,128)S(1)}, u32[]{:S(2)}, u32[]{:S(2)}) collective-permute-start(f32[3,256]{1,0:T(4,128)S(1)} %get-tuple-element.181), channel_id=1, source_target_pairs={{2,0},{4,2},{6,4},{8,6},{10,8},{12,10},{14,12},{16,14},{18,16},{20... | collective-permute-start | bytes 9224 | tf_op jit(solution)/shard_map/while/body/eval_jaxpr/ppermute | solution.py:10
  198.6 11.4 %collective-permute-start = (f32[256,512]{1,0:T(8,128)S(1)}, f32[256,512]{1,0:T(8,128)S(1)}, u32[]{:S(2)}, u32[]{:S(2)}) collective-permute-start(f32[256,512]{1,0:T(8,128)S(1)} %get-tuple-element.180), channel_id=1, source_target_pairs={{2,0},{4,2},{6,4},{8,6},{10,8},{12,10},{14,12},{16,14},{18,16},{20... | collective-permute-start | bytes 1572872 | tf_op jit(solution)/shard_map/while/body/eval_jaxpr/ppermute | solution.py:10
  204.5 5.4 %collective-permute-start.1 = (f32[3,256]{1,0:T(4,128)S(1)}, f32[3,256]{1,0:T(4,128)S(1)}, u32[]{:S(2)}, u32[]{:S(2)}) collective-permute-start(f32[3,256]{1,0:T(4,128)S(1)} %get-tuple-element.181), channel_id=1, source_target_pairs={{2,0},{4,2},{6,4},{8,6},{10,8},{12,10},{14,12},{16,14},{18,16},{20... | collective-permute-start | bytes 9224 | tf_op jit(solution)/shard_map/while/body/eval_jaxpr/ppermute | solution.py:10
  212.3 1.0 copy-start
  213.3 143.6 %all-reduce.6.cloned.1.call-start = ((), (), s32[]{:S(2)}) async-start(), calls=%async_computation.1 | async-start | bytes 2097152 | tf_op jit(solution)/shard_map/psum | solution.py:50
  358.2 1.2 copy-start.2
  443.2 48.0 %copy-start.1 = (f32[512,512]{1,0:T(8,128)S(1)}, f32[512,512]{1,0:T(8,128)}, u32[]{:S(2)}) copy-start(f32[512,512]{1,0:T(8,128)} %all-reduce.4.cloned.1.call-done) | copy-start | bytes 3145732
Sparse Core Ops, SparseCore 0:
  213.4 46.6 all-reduce.3
  264.3 92.5 all-reduce.5
where the time goes:
time: 510 us; the launch traced here: 505 us
  waiting for transfers between devices  155 us (30%)
  starting transfers between devices  150 us (29%)
  other arithmetic  120 us (24%)
  matrix products  46.4 us (9%)
  between operations  16.7 us (3%)
  local copies, waits for them, and re-layouts  15.4 us (3%)
    ppermute x30, starting transfers between devices, shifted(): return lax.ppermute(block, axis, route)  150 us
    psum x1, waiting for transfers between devices, shards(): correlation = lax.psum(partial_correlation, 'blk')  92.7 us
    another operation x14, other arithmetic, shards(): factor = jnp.linalg.cholesky(-correlation)  78.9 us
    psum x1, waiting for transfers between devices, shards(): applied = lax.psum(applied, 'grp')  46.6 us
    another operation x4, other arithmetic, shards(): lax.linalg.triangular_solve(factor, applied, left_side=False, lower=True,...  39.5 us
    dot_general x16, matrix products, tile(): return applied - weight * jnp.dot(screened, far_rows, precision=highest)  19.3 us
    dot_general x16, matrix products, tile(): lax.dot_general(orbitals, far_rows, (((1,), (1,)), ((), ())), precision=h...  16.5 us
    ppermute x30, waiting for transfers between devices, shifted(): return lax.ppermute(block, axis, route)  16 us
  transfers between devices with their start and end apart: 32, of which 17 were waited for; matrix products, arithmetic and copies ran while one was open for 0% of the time, Pallas kernels for 0%

commit v1 on v0

v1 whole, which is shorter than its diff:
```python
import functools

import jax
import jax.numpy as jnp
from jax import lax
from jax.experimental import pallas as pl
from jax.experimental.pallas import tpu as pltpu
from jax.sharding import PartitionSpec as P

MESH = pl.DeviceIdType.MESH
F32 = jnp.float32
BF16 = jnp.bfloat16
HIGHEST = lax.Precision.HIGHEST
PAD = 8


def two_wide(mesh):
    devices = mesh.devices.reshape(mesh.shape["blk"], mesh.shape["grp"])
    if devices.shape[0] < 6:
        return True
    near = getattr(devices[0, 0], "coords", None)
    far = getattr(devices[4, 0], "coords", None)
    if near is None or far is None:
        return True
    return sum(abs(a - b) for a, b in zip(near, far)) == 1


def split(value):
    high = value.astype(BF16)
    return high, (value - high.astype(F32)).astype(BF16)


def dot(a, b, dims):
    return lax.dot_general(a, b, (dims, ((), ())), preferred_element_type=F32)


def dot3(a, b, dims):
    return dot(a[0], b[0], dims) + (dot(a[1], b[0], dims) + dot(a[0], b[1], dims))


def apply_kernel(
    sizes, orb_ref, own_ref, near_ref, applied_ref, corr_ref,
    buf, nh, nl, th, tl, fh, fl, acc, part, half_buf, red, rs_buf, grp_buf, corr_buf, app_buf,
    gather_recv, gather_send, half_sem, rs_send, rs_recv, grp_send, grp_recv,
    ag_recv, ag_send, ag_sib, app_send, app_recv,
):
    n_blk, n_grp, inner_two, weight, tile = sizes
    chips = n_blk // 2
    length = chips // 2
    rows, norb = orb_ref.shape
    piece = own_ref.shape[1] - PAD
    width = 2 * piece
    me = lax.axis_index("blk")
    grp = lax.axis_index("grp")
    core = me % 2
    chip = me // 2

    def chip_at(position):
        side = position // length
        along = side * (2 * length - 1 - 2 * position) + position
        return along * 2 + side if inner_two else side * length + along

    if inner_two:
        side, along = chip % 2, chip // 2
    else:
        side, along = chip // length, chip % length
    place = along + side * (2 * length - 1 - 2 * along)

    def device_at(position, which):
        return chip_at((position + 2 * chips) % chips) * 2 + which

    sibling = me + 1 - 2 * core
    right = device_at(place + 1, core)
    left = device_at(place - 1, core)

    def send(origin, h, kind, target):
        return pltpu.make_async_remote_copy(
            src_ref=buf.at[origin, h], dst_ref=buf.at[origin, h],
            send_sem=gather_send.at[kind, origin, h], recv_sem=gather_recv.at[origin, h],
            device_id={"blk": target}, device_id_type=MESH)

    def arrived(origin, h):
        send(origin, h, 0, right).wait_recv()

    barrier = pltpu.get_barrier_semaphore()
    pl.semaphore_signal(barrier, inc=1, device_id={"blk": sibling}, device_id_type=MESH)
    for j in range(1, chips):
        pl.semaphore_signal(barrier, inc=1, device_id={"blk": device_at(place + j, core)}, device_id_type=MESH)
    for j in range(1, n_grp):
        pl.semaphore_signal(barrier, inc=1, device_id={"grp": (grp + j) % n_grp}, device_id_type=MESH)
    buf[me] = own_ref[...]
    pl.semaphore_wait(barrier, 1 + (chips - 1) + (n_grp - 1))

    for h in range(2):
        send(me, h, 0, right).start()
        send(me, h, 1, left).start()
        send(me, h, 2, sibling).start()

    near_high, near_low = split(orb_ref[...])
    nh[...] = near_high
    nl[...] = near_low
    turned_high, turned_low = split(orb_ref[...].T)
    th[...] = turned_high
    tl[...] = turned_low
    acc[...] = jnp.zeros_like(acc)

    def compute(origin):
        for h in range(2):
            high, low = split(buf[origin, h, :piece, :])
            fh[h * piece:(h + 1) * piece, :] = high
            fl[h * piece:(h + 1) * piece, :] = low
        coords = buf[origin, 0, piece:, :width]
        far = (fh[...], fl[...])

        def rows_of(t, carry):
            here = pl.ds(pl.multiple_of(t * tile, tile), tile)
            gram = dot3((nh[here, :], nl[here, :]), far, ((1,), (1,)))
            squared = jnp.zeros((tile, width), F32)
            for k in range(3):
                spacing = near_ref[here, k:k + 1] - coords[k:k + 1, :]
                squared = squared + spacing * spacing
            screened = split(gram * lax.rsqrt(squared + 0.0025))
            acc[here, :] += dot3(screened, far, ((1,), (0,)))
            return carry

        lax.fori_loop(0, rows // tile, rows_of, 0)

    def first(i, carry):
        origin = jnp.where(i == 0, me, sibling)

        @pl.when(i == 1)
        def _():
            arrived(sibling, 0)
            arrived(sibling, 1)

        compute(origin)
        return carry

    lax.fori_loop(0, 2, first, 0)

    full = (chips - 1) // 2

    def service(d, h):
        for kind, sign, target in ((0, -1, right), (1, 1, left)):
            origin = device_at(place + sign * d, core)
            arrived(origin, h)
            if h == kind:
                send(origin, h, kind, target).start()
            else:
                @pl.when(d < full)
                def _():
                    send(origin, h, kind, target).start()
            send(origin, h, 2, sibling).start()

    def pair(d, which, wait):
        def one(i, carry):
            origin = device_at(place + (2 * i - 1) * d, which)
            if wait:
                arrived(origin, 0)
                arrived(origin, 1)
            compute(origin)
            return carry
        lax.fori_loop(0, 2, one, 0)

    def round_of(d, carry):
        service(d, 0)

        @pl.when(d > 1)
        def _():
            pair(d - 1, 1 - core, True)

        service(d, 1)
        pair(d, core, False)
        return carry

    lax.fori_loop(1, full + 1, round_of, 0)
    pair(full, 1 - core, True)
    across = device_at(place + length, core)
    for h in range(2):
        arrived(across, h)
        send(across, h, 2, sibling).start()

    def last(i, carry):
        origin = device_at(place + length, jnp.where(i == 0, core, 1 - core))

        @pl.when(i == 1)
        def _():
            arrived(origin, 0)
            arrived(origin, 1)

        compute(origin)
        return carry

    lax.fori_loop(0, 2, last, 0)

    app_buf[grp] = -weight * acc[...]

    def app_copy(j):
        return pltpu.make_async_remote_copy(
            src_ref=app_buf.at[grp], dst_ref=app_buf.at[grp],
            send_sem=app_send.at[j], recv_sem=app_recv.at[grp],
            device_id={"grp": (grp + j) % n_grp}, device_id_type=MESH)

    def app_in(j):
        other = (grp + j) % n_grp
        return pltpu.make_async_remote_copy(
            src_ref=app_buf.at[other], dst_ref=app_buf.at[other],
            send_sem=app_send.at[j], recv_sem=app_recv.at[other],
            device_id={"grp": other}, device_id_type=MESH)

    half = norb // 2
    share = half // chips
    scaled = split(acc[...])
    part[...] = (dot3((th[...], tl[...]), scaled, ((1,), (0,))) * (weight * weight)).reshape(part.shape)
    to_sibling = pltpu.make_async_remote_copy(
        src_ref=part.at[1 - core], dst_ref=half_buf, send_sem=half_sem.at[0], recv_sem=half_sem.at[1],
        device_id={"blk": sibling}, device_id_type=MESH)
    to_sibling.start()
    for j in range(1, n_grp):
        app_copy(j).start()
    to_sibling.wait_recv()
    red[...] = (part[core] + half_buf[...]).reshape(red.shape)

    def rs_copy(j):
        to = (place + j) % chips
        return pltpu.make_async_remote_copy(
            src_ref=red.at[to], dst_ref=rs_buf.at[j], send_sem=rs_send.at[j], recv_sem=rs_recv.at[j],
            device_id={"blk": device_at(to, core)}, device_id_type=MESH)

    for j in range(1, chips):
        rs_copy(j).start()
    total = red[place]
    for j in range(1, chips):
        rs_copy(j).wait_recv()
        total = total + rs_buf[j]
    grp_buf[grp] = total

    def grp_copy(j):
        return pltpu.make_async_remote_copy(
            src_ref=grp_buf.at[grp], dst_ref=grp_buf.at[grp],
            send_sem=grp_send.at[j], recv_sem=grp_recv.at[grp],
            device_id={"grp": (grp + j) % n_grp}, device_id_type=MESH)

    def grp_in(j):
        other = (grp + j) % n_grp
        return pltpu.make_async_remote_copy(
            src_ref=grp_buf.at[other], dst_ref=grp_buf.at[other],
            send_sem=grp_send.at[j], recv_sem=grp_recv.at[other],
            device_id={"grp": other}, device_id_type=MESH)

    for j in range(1, n_grp):
        grp_copy(j).start()
    for j in range(1, n_grp):
        grp_in(j).wait_recv()
    total = grp_buf[0]
    for j in range(1, n_grp):
        total = total + grp_buf[j]
    mine = core * chips + place
    corr_buf[mine] = total

    def ag_copy(block, sem, target):
        return pltpu.make_async_remote_copy(
            src_ref=corr_buf.at[block], dst_ref=corr_buf.at[block],
            send_sem=sem, recv_sem=ag_recv.at[block],
            device_id={"blk": target}, device_id_type=MESH)

    for j in range(1, chips):
        ag_copy(mine, ag_send.at[j], device_at(place + j, core)).start()
    ag_copy(mine, ag_sib.at[0], sibling).start()
    for j in range(1, chips):
        block = core * chips + (place + chips - j) % chips
        ag_copy(block, ag_sib.at[j], sibling).wait_recv()
        ag_copy(block, ag_sib.at[j], sibling).start()
    for j in range(chips):
        block = (1 - core) * chips + (place + chips - j) % chips
        ag_copy(block, ag_sib.at[j], sibling).wait_recv()
    corr_ref[...] = corr_buf[...]

    for j in range(1, n_grp):
        app_in(j).wait_recv()
    whole = app_buf[0]
    for j in range(1, n_grp):
        whole = whole + app_buf[j]
    applied_ref[...] = whole

    def sent(d, carry):
        for kind, sign, target in ((0, -1, right), (1, 1, left)):
            origin = device_at(place + sign * d, core)
            for h in range(2):
                if h == kind:
                    send(origin, h, kind, target).wait_send()
                else:
                    @pl.when(d < full)
                    def _():
                        send(origin, h, kind, target).wait_send()
                send(origin, h, 2, sibling).wait_send()
        return carry

    lax.fori_loop(1, full + 1, sent, 0)
    for h in range(2):
        send(me, h, 0, right).wait_send()
        send(me, h, 1, left).wait_send()
        send(me, h, 2, sibling).wait_send()
        send(across, h, 2, sibling).wait_send()
    to_sibling.wait_send()
    for j in range(1, chips):
        rs_copy(j).wait_send()
        ag_copy(mine, ag_send.at[j], device_at(place + j, core)).wait_send()
    for j in range(chips):
        block = core * chips + (place + chips - j) % chips
        ag_copy(block, ag_sib.at[j], sibling).wait_send()
    for j in range(1, n_grp):
        app_copy(j).wait_send()
        grp_copy(j).wait_send()


def solve_kernel(corr_ref, applied_ref, out_ref, a, work):
    norb = corr_ref.shape[0]
    rows = applied_ref.shape[0]
    base = 128
    a[:norb, :] = corr_ref[...]
    a[norb:, :] = applied_ref[...]
    lane = lax.broadcasted_iota(jnp.int32, (8, base), 1)
    sub = lax.broadcasted_iota(jnp.int32, (8, base), 0)
    eye = (lax.broadcasted_iota(jnp.int32, (base, base), 0)
           == lax.broadcasted_iota(jnp.int32, (base, base), 1)).astype(F32)
    for b in range(norb // base):
        here = slice(b * base, (b + 1) * base)
        work[:, :base] = a[here, here]
        work[:, base:] = eye

        def slab(s, carry):
            top = pl.multiple_of(s * 8, 8)
            left = work[pl.ds(top, 8), :base]
            right = work[pl.ds(top, 8), base:]
            rolled = pltpu.roll(left, base - s * 8, axis=1)
            cols = [jnp.broadcast_to(rolled[:, j:j + 1], (8, base)) for j in range(8)]
            scale = jnp.zeros((8, base), F32)
            for j in range(8):
                pivot = jnp.broadcast_to(cols[j][j:j + 1, :], (8, base))
                root = lax.rsqrt(pivot)
                scale = jnp.where(sub == j, root, scale)
                factor = jnp.where(sub > j, cols[j] / pivot, 0.0)
                left = left - factor * left[j:j + 1, :]
                right = right - factor * right[j:j + 1, :]
                for m in range(j + 1, 8):
                    cols[m] = cols[m] - factor * cols[m][j:j + 1, :]
            left = left * scale
            right = right * scale
            work[pl.ds(top, 8), base:] = right
            below = jnp.where(lane >= s * 8 + 8, left, 0.0)
            both = jnp.concatenate([left, right], axis=1)
            work[...] -= lax.dot_general(
                below, both, (((0,), (0,)), ((), ())), precision=HIGHEST, preferred_element_type=F32)
            return carry

        lax.fori_loop(0, base // 8, slab, 0)
        inverse = work[:, base:]
        below = slice((b + 1) * base, norb + rows)
        panel = lax.dot_general(
            a[below, here], inverse, (((1,), (1,)), ((), ())), precision=HIGHEST, preferred_element_type=F32)
        a[below, here] = panel
        for j in range(b + 1, norb // base):
            there = slice(j * base, (j + 1) * base)
            low = slice(j * base, norb + rows)
            a[low, there] -= lax.dot_general(
                a[low, here], a[there, here], (((1,), (1,)), ((), ())),
                precision=HIGHEST, preferred_element_type=F32)
    out_ref[...] = a[norb:, :]


def solution(mesh):
    n_blk, n_grp = mesh.shape["blk"], mesh.shape["grp"]
    inner_two = two_wide(mesh)
    chips = n_blk // 2

    def shards(orbitals, points):
        rows, norb = orbitals.shape
        weight = 1.0 / (rows * n_blk)
        width = rows // n_grp
        piece = width // 2
        start = lax.axis_index("grp") * width
        far_rows = lax.dynamic_slice_in_dim(orbitals, start, width, 0).reshape(2, piece, norb)
        far_coords = lax.dynamic_slice_in_dim(points, start, width, 1)
        far_coords = jnp.pad(far_coords, ((0, PAD - 3), (0, norb - width)))
        own = jnp.concatenate([far_rows, jnp.broadcast_to(far_coords, (2, PAD, norb))], axis=1)
        share = norb // 2 // chips
        vmem = pl.BlockSpec(memory_space=pltpu.VMEM)
        dma = pltpu.SemaphoreType.DMA
        applied, corr = pl.pallas_call(
            functools.partial(apply_kernel, (n_blk, n_grp, inner_two, weight, min(256, rows))),
            out_shape=[jax.ShapeDtypeStruct((rows, norb), F32), jax.ShapeDtypeStruct((n_blk, share, norb), F32)],
            in_specs=[vmem] * 3,
            out_specs=[vmem] * 2,
            scratch_shapes=[
                pltpu.VMEM((n_blk, 2, piece + PAD, norb), F32),
                pltpu.VMEM((rows, norb), BF16), pltpu.VMEM((rows, norb), BF16),
                pltpu.VMEM((norb, rows), BF16), pltpu.VMEM((norb, rows), BF16),
                pltpu.VMEM((width, norb), BF16), pltpu.VMEM((width, norb), BF16),
                pltpu.VMEM((rows, norb), F32),
                pltpu.VMEM((2, norb // 2, norb), F32),
                pltpu.VMEM((norb // 2, norb), F32),
                pltpu.VMEM((chips, share, norb), F32),
                pltpu.VMEM((chips, share, norb), F32),
                pltpu.VMEM((n_grp, share, norb), F32),
                pltpu.VMEM((n_blk, share, norb), F32),
                pltpu.VMEM((n_grp, rows, norb), F32),
                dma((n_blk, 2)), dma((3, n_blk, 2)), dma((2,)), dma((chips,)), dma((chips,)),
                dma((n_grp,)), dma((n_grp,)), dma((n_blk,)), dma((chips,)), dma((chips,)),
                dma((n_grp,)), dma((n_grp,)),
            ],
            compiler_params=pltpu.CompilerParams(
                collective_id=0, has_side_effects=True, vmem_limit_bytes=48 << 20),
            name="apply_and_correlate",
        )(orbitals, own, points.T)
        return pl.pallas_call(
            solve_kernel,
            out_shape=jax.ShapeDtypeStruct((rows, norb), F32),
            in_specs=[vmem] * 2,
            out_specs=vmem,
            scratch_shapes=[pltpu.VMEM((norb + rows, norb), F32), pltpu.VMEM((128, 256), F32)],
            compiler_params=pltpu.CompilerParams(vmem_limit_bytes=32 << 20),
            name="factor_and_solve",
        )(corr.reshape(norb, norb), applied)

    return jax.shard_map(
        shards,
        mesh=mesh,
        in_specs=(P("blk", None), P(None, "blk")),
        out_specs=P("blk", None),
        check_vma=False,
    )
```

time: 510 us -> 143 us (0.28); the launches traced: 505 us -> 143 us
  waiting for transfers between devices: 155 us -> 0 us
  starting transfers between devices: 150 us -> 0 us
  Pallas kernels: 0 us -> 141 us
  other arithmetic: 120 us -> 0.04 us
  matrix products: 46.4 us -> 0 us
  between operations: 16.7 us -> 0.04 us
  local copies, waits for them, and re-layouts: 15.4 us -> 2.19 us
    ppermute x30 -> x0, starting transfers between devices: 150 us -> none  [shifted(): return lax.ppermute(block, axis, route)]
    pallas_call x0 -> x2, Pallas kernels: none -> 141 us  [the longest x1 99 us: shards(): pl.pallas_call(functools.partial(apply_kernel, (n_blk, n_grp, inner_two,...]
    psum x2 -> x0, waiting for transfers between devices: 139 us -> none  [the longest x1 92.7 us: shards(): correlation = lax.psum(partial_correlation, 'blk')]
    another operation x18 -> x0, other arithmetic: 118 us -> none  [the longest x14 78.9 us: shards(): factor = jnp.linalg.cholesky(-correlation)]
    dot_general x33 -> x0, matrix products: 39.8 us -> none  [the longest x16 19.3 us: tile(): return applied - weight * jnp.dot(screened, far_rows, precision=highest)]
    ppermute x30 -> x0, waiting for transfers between devices: 16 us -> none  [shifted(): return lax.ppermute(block, axis, route)]
    another operation x18 -> x0, local copies, waits for them, and re-layouts: 9.84 us -> none
    another operation x13 -> x0, matrix products: 6.62 us -> none  [the longest x7 4.75 us: shards(): lax.linalg.triangular_solve(factor, applied, left_side=False, lower=True,...]
  transfers between devices with their start and end apart: 32 -> 0, of which waited for: 17 -> 0; matrix products, arithmetic and copies ran while one was open for 0% -> 0% of each run, Pallas kernels for 0% -> 0%
where the time goes in v1:
time: 143 us
  Pallas kernels  141 us (99%)
  local copies, waits for them, and re-layouts  2.19 us (2%)
    pallas_call x1, Pallas kernels, shards(): pl.pallas_call(functools.partial(apply_kernel, (n_blk, n_grp, inner_two,...  99 us
    pallas_call x1, Pallas kernels, shards(): pl.pallas_call(solve_kernel, out_shape=jax.ShapeDtypeStruct((rows, norb),...  41.8 us

profile of v1, /device:TPU:1, one launch (start us, length us, event | category | flops | bytes accessed | tf_op | source)
XLA Modules:
  0.0 143.1 jit_solution(6792618006550010943)
XLA Ops:
  0.0 0.0 copy-start.1
  0.0 0.7 copy-done.1
  0.7 0.1 copy.3
  0.9 0.0 copy-start
  0.9 1.2 constant_dynamic-slice_fusion.1
  2.1 0.2 copy-done
  2.3 99.0 %apply_and_correlate.1 = (f32[512,512]{1,0:T(8,128)S(1)}, f32[16,32,512]{2,1,0:T(8,128)S(1)}) custom-call(f32[512,512]{1,0:T(8,128)S(1)} %copy-done, f32[2,136,512]{2,1,0:T(8,128)S(1)} %pad_maximum_fusion.own_ref, f32[512,3]{1,0:T(8,128)S(1)} %bitcast.4), custom_call_target="tpu_custom_call" | custom-call | tf_op jit(solution)/shard_map/apply_and_correlate/pallas_call | solution.py:390
  101.3 41.8 %factor_and_solve.1 = f32[512,512]{1,0:T(8,128)} custom-call(f32[512,512]{1,0:T(8,128)S(1)} %bitcast.3, f32[512,512]{1,0:T(8,128)S(1)} %get-tuple-element.8.applied_ref), custom_call_target="tpu_custom_call" | custom-call | tf_op jit(solution)/shard_map/factor_and_solve/pallas_call | solution.py:416
  (4 shorter events, 0.1 us)
Async XLA Ops:
  0.0 0.7 copy-start.1
  0.9 1.4 copy-start

commit v2 on v1

--- a/solution.py
+++ b/solution.py
@@ -12,6 +12,7 @@
 BF16 = jnp.bfloat16
 HIGHEST = lax.Precision.HIGHEST
 PAD = 8
+BASE = 128
 
 
 def two_wide(mesh):
@@ -40,7 +41,7 @@
 
 def apply_kernel(
     sizes, orb_ref, own_ref, near_ref, applied_ref, corr_ref,
-    buf, nh, nl, th, tl, fh, fl, acc, part, half_buf, red, rs_buf, grp_buf, corr_buf, app_buf,
+    buf, near3, turned3, far3, low3, acc, part, half_buf, red, rs_buf, grp_buf, corr_buf, app_buf,
     gather_recv, gather_send, half_sem, rs_send, rs_recv, grp_send, grp_recv,
     ag_recv, ag_send, ag_sib, app_send, app_recv,
 ):
@@ -97,30 +98,34 @@
         send(me, h, 2, sibling).start()
 
     near_high, near_low = split(orb_ref[...])
-    nh[...] = near_high
-    nl[...] = near_low
     turned_high, turned_low = split(orb_ref[...].T)
-    th[...] = turned_high
-    tl[...] = turned_low
+    for k, (near_part, turned_part) in enumerate(
+            ((near_high, turned_high), (near_low, turned_low), (near_high, turned_high))):
+        near3[:, k * norb:(k + 1) * norb] = near_part
+        turned3[:, k * rows:(k + 1) * rows] = turned_part
     acc[...] = jnp.zeros_like(acc)
 
     def compute(origin):
         for h in range(2):
             high, low = split(buf[origin, h, :piece, :])
-            fh[h * piece:(h + 1) * piece, :] = high
-            fl[h * piece:(h + 1) * piece, :] = low
+            for k, far_part in enumerate((high, high, low)):
+                far3[h * piece:(h + 1) * piece, k * norb:(k + 1) * norb] = far_part
+                low3[k * width + h * piece:k * width + (h + 1) * piece, :] = far_part
         coords = buf[origin, 0, piece:, :width]
-        far = (fh[...], fl[...])
 
         def rows_of(t, carry):
             here = pl.ds(pl.multiple_of(t * tile, tile), tile)
-            gram = dot3((nh[here, :], nl[here, :]), far, ((1,), (1,)))
+            gram = dot(near3[here, :], far3[...], ((1,), (1,)))
             squared = jnp.zeros((tile, width), F32)
             for k in range(3):
                 spacing = near_ref[here, k:k + 1] - coords[k:k + 1, :]
                 squared = squared + spacing * spacing
-            screened = split(gram * lax.rsqrt(squared + 0.0025))
-            acc[here, :] += dot3(screened, far, ((1,), (0,)))
+            high, low = split(gram * lax.rsqrt(squared + 0.0025))
+            if width % 128 == 0:
+                acc[here, :] += dot(jnp.concatenate([high, low, high], axis=1), low3[...], ((1,), (0,)))
+            else:
+                top, bottom = low3[:width, :], low3[2 * width:, :]
+                acc[here, :] += dot3((high, low), (top, bottom), ((1,), (0,)))
             return carry
 
         lax.fori_loop(0, rows // tile, rows_of, 0)
@@ -208,10 +213,15 @@
             send_sem=app_send.at[j], recv_sem=app_recv.at[other],
             device_id={"grp": other}, device_id_type=MESH)
 
-    half = norb // 2
-    share = half // chips
-    scaled = split(acc[...])
-    part[...] = (dot3((th[...], tl[...]), scaled, ((1,), (0,))) * (weight * weight)).reshape(part.shape)
+    high, low = split(acc[...])
+    scaled3 = jnp.concatenate([high, high, low], axis=0)
+    blocks = [(i, j) for i in range(norb // BASE) for j in range(i + 1)]
+    for i in range(norb // BASE):
+        made = dot(turned3[i * BASE:(i + 1) * BASE, :], scaled3[:, :(i + 1) * BASE], ((1,), (0,)))
+        made = made * (weight * weight)
+        for j in range(i + 1):
+            side_of, index = divmod(blocks.index((i, j)), len(blocks) // 2)
+            part[side_of, index * BASE:(index + 1) * BASE, :] = made[:, j * BASE:(j + 1) * BASE]
     to_sibling = pltpu.make_async_remote_copy(
         src_ref=part.at[1 - core], dst_ref=half_buf, send_sem=half_sem.at[0], recv_sem=half_sem.at[1],
         device_id={"blk": sibling}, device_id_type=MESH)
@@ -314,52 +324,78 @@
         grp_copy(j).wait_send()
 
 
+def split3(value):
+    high = value.astype(BF16).astype(F32)
+    rest = value - high
+    middle = rest.astype(BF16).astype(F32)
+    return high, middle, rest - middle
+
+
+def diagonal_inverse(work):
+    size = work.shape[0]
+    sub = lax.broadcasted_iota(jnp.int32, (8, size), 0)
+    lane = lax.broadcasted_iota(jnp.int32, (8, size), 1)
+
+    def eliminate(top, both):
+        count = 2 if both else 1
+        left = [work[top + 8 * r:top + 8 * r + 8, :size] for r in range(count)]
+        right = [work[top + 8 * r:top + 8 * r + 8, size:] for r in range(count)]
+        cols = [[jnp.broadcast_to(left[r][:, top + j:top + j + 1], (8, size)) for j in range(8)] for r in range(count)]
+        scale = jnp.ones((8, size), F32)
+        for j in range(8):
+            root = lax.rsqrt(jnp.broadcast_to(cols[0][j][j:j + 1, :], (8, size)))
+            scale = jnp.where(sub == j, root, scale)
+            inverse = root * root
+            left_row, right_row = left[0][j:j + 1, :], right[0][j:j + 1, :]
+            col_rows = [cols[0][m][j:j + 1, :] for m in range(8)]
+            for r in range(count):
+                factor = cols[r][j] * inverse
+                if r == 0:
+                    factor = jnp.where(sub > j, factor, 0.0)
+                for m in range(j + 1, 8):
+                    cols[r][m] = cols[r][m] - factor * col_rows[m]
+                left[r] = left[r] - factor * left_row
+                right[r] = right[r] - factor * right_row
+        pivots_left, pivots_right = left[0] * scale, right[0] * scale
+        work[top:top + 8, size:] = pivots_right
+        if both:
+            work[top + 8:top + 16, :size] = left[1]
+            work[top + 8:top + 16, size:] = right[1]
+        rest = top + 16
+        if rest < size:
+            below = jnp.where(lane >= rest, pivots_left, 0.0)
+            bh, bm, bl = split3(below)
+            ah, am, al = split3(jnp.concatenate([pivots_left, pivots_right], axis=1))
+            near = jnp.concatenate([bh, bh, bm, bh, bl, bm], axis=0).astype(BF16)
+            far = jnp.concatenate([ah, am, ah, al, ah, am], axis=0).astype(BF16)
+            update = dot(near, far, ((0,), (0,)))
+            work[rest:, :] -= update[rest:, :]
+
+    for step in range(size // 8):
+        eliminate(8 * step, 8 * step + 8 < size)
+
+
 def solve_kernel(corr_ref, applied_ref, out_ref, a, work):
-    norb = corr_ref.shape[0]
+    norb = applied_ref.shape[1]
     rows = applied_ref.shape[0]
-    base = 128
-    a[:norb, :] = corr_ref[...]
+    base = BASE
+    index = 0
+    for i in range(norb // base):
+        for j in range(i + 1):
+            a[i * base:(i + 1) * base, j * base:(j + 1) * base] = corr_ref[index * base:(index + 1) * base, :]
+            index += 1
     a[norb:, :] = applied_ref[...]
-    lane = lax.broadcasted_iota(jnp.int32, (8, base), 1)
-    sub = lax.broadcasted_iota(jnp.int32, (8, base), 0)
     eye = (lax.broadcasted_iota(jnp.int32, (base, base), 0)
            == lax.broadcasted_iota(jnp.int32, (base, base), 1)).astype(F32)
     for b in range(norb // base):
         here = slice(b * base, (b + 1) * base)
         work[:, :base] = a[here, here]
         work[:, base:] = eye
-
-        def slab(s, carry):
-            top = pl.multiple_of(s * 8, 8)
-            left = work[pl.ds(top, 8), :base]
-            right = work[pl.ds(top, 8), base:]
-            rolled = pltpu.roll(left, base - s * 8, axis=1)
-            cols = [jnp.broadcast_to(rolled[:, j:j + 1], (8, base)) for j in range(8)]
-            scale = jnp.zeros((8, base), F32)
-            for j in range(8):
-                pivot = jnp.broadcast_to(cols[j][j:j + 1, :], (8, base))
-                root = lax.rsqrt(pivot)
-                scale = jnp.where(sub == j, root, scale)
-                factor = jnp.where(sub > j, cols[j] / pivot, 0.0)
-                left = left - factor * left[j:j + 1, :]
-                right = right - factor * right[j:j + 1, :]
-                for m in range(j + 1, 8):
-                    cols[m] = cols[m] - factor * cols[m][j:j + 1, :]
-            left = left * scale
-            right = right * scale
-            work[pl.ds(top, 8), base:] = right
-            below = jnp.where(lane >= s * 8 + 8, left, 0.0)
-            both = jnp.concatenate([left, right], axis=1)
-            work[...] -= lax.dot_general(
-                below, both, (((0,), (0,)), ((), ())), precision=HIGHEST, preferred_element_type=F32)
-            return carry
-
-        lax.fori_loop(0, base // 8, slab, 0)
+        diagonal_inverse(work)
         inverse = work[:, base:]
         below = slice((b + 1) * base, norb + rows)
-        panel = lax.dot_general(
+        a[below, here] = lax.dot_general(
             a[below, here], inverse, (((1,), (1,)), ((), ())), precision=HIGHEST, preferred_element_type=F32)
-        a[below, here] = panel
         for j in range(b + 1, norb // base):
             there = slice(j * base, (j + 1) * base)
             low = slice(j * base, norb + rows)
@@ -384,26 +420,28 @@
         far_coords = lax.dynamic_slice_in_dim(points, start, width, 1)
         far_coords = jnp.pad(far_coords, ((0, PAD - 3), (0, norb - width)))
         own = jnp.concatenate([far_rows, jnp.broadcast_to(far_coords, (2, PAD, norb))], axis=1)
-        share = norb // 2 // chips
+        packed = norb * (norb // BASE + 1) // 2
+        share = packed // n_blk
         vmem = pl.BlockSpec(memory_space=pltpu.VMEM)
         dma = pltpu.SemaphoreType.DMA
         applied, corr = pl.pallas_call(
             functools.partial(apply_kernel, (n_blk, n_grp, inner_two, weight, min(256, rows))),
-            out_shape=[jax.ShapeDtypeStruct((rows, norb), F32), jax.ShapeDtypeStruct((n_blk, share, norb), F32)],
+            out_shape=[jax.ShapeDtypeStruct((rows, norb), F32), jax.ShapeDtypeStruct((n_blk, share, BASE), F32)],
             in_specs=[vmem] * 3,
             out_specs=[vmem] * 2,
             scratch_shapes=[
                 pltpu.VMEM((n_blk, 2, piece + PAD, norb), F32),
-                pltpu.VMEM((rows, norb), BF16), pltpu.VMEM((rows, norb), BF16),
-                pltpu.VMEM((norb, rows), BF16), pltpu.VMEM((norb, rows), BF16),
-                pltpu.VMEM((width, norb), BF16), pltpu.VMEM((width, norb), BF16),
+                pltpu.VMEM((rows, 3 * norb), BF16),
+                pltpu.VMEM((norb, 3 * rows), BF16),
+                pltpu.VMEM((width, 3 * norb), BF16),
+                pltpu.VMEM((3 * width, norb), BF16),
                 pltpu.VMEM((rows, norb), F32),
-                pltpu.VMEM((2, norb // 2, norb), F32),
-                pltpu.VMEM((norb // 2, norb), F32),
-                pltpu.VMEM((chips, share, norb), F32),
-                pltpu.VMEM((chips, share, norb), F32),
-                pltpu.VMEM((n_grp, share, norb), F32),
-                pltpu.VMEM((n_blk, share, norb), F32),
+                pltpu.VMEM((2, packed // 2, BASE), F32),
+                pltpu.VMEM((packed // 2, BASE), F32),
+                pltpu.VMEM((chips, share, BASE), F32),
+                pltpu.VMEM((chips, share, BASE), F32),
+                pltpu.VMEM((n_grp, share, BASE), F32),
+                pltpu.VMEM((n_blk, share, BASE), F32),
                 pltpu.VMEM((n_grp, rows, norb), F32),
                 dma((n_blk, 2)), dma((3, n_blk, 2)), dma((2,)), dma((chips,)), dma((chips,)),
                 dma((n_grp,)), dma((n_grp,)), dma((n_blk,)), dma((chips,)), dma((chips,)),
@@ -421,7 +459,7 @@
             scratch_shapes=[pltpu.VMEM((norb + rows, norb), F32), pltpu.VMEM((128, 256), F32)],
             compiler_params=pltpu.CompilerParams(vmem_limit_bytes=32 << 20),
             name="factor_and_solve",
-        )(corr.reshape(norb, norb), applied)
+        )(corr.reshape(packed, BASE), applied)
 
     return jax.shard_map(
         shards,

time: 143 us -> 118 us (0.83)
  Pallas kernels: 141 us -> 116 us
    pallas_call x1, Pallas kernels: 41.8 us -> 21.1 us  [shards(): pl.pallas_call(solve_kernel, out_shape=jax.ShapeDtypeStruct((rows, norb),...]
    pallas_call x1, Pallas kernels: 99 us -> 94.6 us  [shards(): pl.pallas_call(functools.partial(apply_kernel, (n_blk, n_grp, inner_two,...]
where the time goes in v2:
time: 118 us
  Pallas kernels  116 us (98%)
  local copies, waits for them, and re-layouts  2.19 us (2%)
    pallas_call x1, Pallas kernels, shards(): pl.pallas_call(functools.partial(apply_kernel, (n_blk, n_grp, inner_two,...  94.6 us
    pallas_call x1, Pallas kernels, shards(): pl.pallas_call(solve_kernel, out_shape=jax.ShapeDtypeStruct((rows, norb),...  21.1 us

profile of v2, /device:TPU:1, one launch (start us, length us, event | category | flops | bytes accessed | tf_op | source)
XLA Modules:
  0.0 117.9 jit_solution(5410564037049605684)
XLA Ops:
  0.0 0.0 copy-start.1
  0.0 0.7 copy-done.1
  0.7 0.1 copy.3
  0.9 0.0 copy-start
  0.9 1.2 constant_dynamic-slice_fusion.1
  2.1 0.2 copy-done
  2.3 94.6 %apply_and_correlate.1 = (f32[512,512]{1,0:T(8,128)S(1)}, f32[16,80,128]{2,1,0:T(8,128)S(1)}) custom-call(f32[512,512]{1,0:T(8,128)S(1)} %copy-done, f32[2,136,512]{2,1,0:T(8,128)S(1)} %pad_maximum_fusion.own_ref, f32[512,3]{1,0:T(8,128)S(1)} %bitcast.3), custom_call_target="tpu_custom_call" | custom-call | tf_op jit(solution)/shard_map/apply_and_correlate/pallas_call | solution.py:427
  96.8 21.1 %factor_and_solve.1 = f32[512,512]{1,0:T(8,128)} custom-call(f32[1280,128]{1,0:T(8,128)S(1)} %bitcast.4, f32[512,512]{1,0:T(8,128)S(1)} %get-tuple-element.8.applied_ref), custom_call_target="tpu_custom_call" | custom-call | tf_op jit(solution)/shard_map/factor_and_solve/pallas_call | solution.py:454
  (4 shorter events, 0.1 us)
Async XLA Ops:
  0.0 0.7 copy-start.1
  0.9 1.4 %copy-start = (f32[512,512]{1,0:T(8,128)S(1)}, f32[512,512]{1,0:T(8,128)}, u32[]{:S(2)}) copy-start(f32[512,512]{1,0:T(8,128)} %orb_ref.1) | copy-start | bytes 3145732

commit v3 on v2

--- a/solution.py
+++ b/solution.py
@@ -13,6 +13,7 @@
 HIGHEST = lax.Precision.HIGHEST
 PAD = 8
 BASE = 128
+PIECES = 4
 
 
 def two_wide(mesh):
@@ -49,8 +50,8 @@
     chips = n_blk // 2
     length = chips // 2
     rows, norb = orb_ref.shape
-    piece = own_ref.shape[1] - PAD
-    width = 2 * piece
+    width = own_ref.shape[0] - PAD
+    piece = width // PIECES
     me = lax.axis_index("blk")
     grp = lax.axis_index("grp")
     core = me % 2
@@ -75,8 +76,9 @@
     left = device_at(place - 1, core)
 
     def send(origin, h, kind, target):
-        return pltpu.make_async_remote_copy(
-            src_ref=buf.at[origin, h], dst_ref=buf.at[origin, h],
+        place_of = pl.ds(0, PAD + piece) if h == 0 else pl.ds(PAD + h * piece, piece)
+        return pltpu.make_async_remote_copy(
+            src_ref=buf.at[origin, place_of], dst_ref=buf.at[origin, place_of],
             send_sem=gather_send.at[kind, origin, h], recv_sem=gather_recv.at[origin, h],
             device_id={"blk": target}, device_id_type=MESH)
 
@@ -92,7 +94,7 @@
     buf[me] = own_ref[...]
     pl.semaphore_wait(barrier, 1 + (chips - 1) + (n_grp - 1))
 
-    for h in range(2):
+    for h in range(PIECES):
         send(me, h, 0, right).start()
         send(me, h, 1, left).start()
         send(me, h, 2, sibling).start()
@@ -106,12 +108,11 @@
     acc[...] = jnp.zeros_like(acc)
 
     def compute(origin):
-        for h in range(2):
-            high, low = split(buf[origin, h, :piece, :])
-            for k, far_part in enumerate((high, high, low)):
-                far3[h * piece:(h + 1) * piece, k * norb:(k + 1) * norb] = far_part
-                low3[k * width + h * piece:k * width + (h + 1) * piece, :] = far_part
-        coords = buf[origin, 0, piece:, :width]
+        high, low = split(buf[origin, PAD:, :])
+        for k, far_part in enumerate((high, high, low)):
+            far3[:, k * norb:(k + 1) * norb] = far_part
+            low3[k * width:(k + 1) * width, :] = far_part
+        coords = buf[origin, :PAD, :width]
 
         def rows_of(t, carry):
             here = pl.ds(pl.multiple_of(t * tile, tile), tile)
@@ -130,73 +131,77 @@
 
         lax.fori_loop(0, rows // tile, rows_of, 0)
 
-    def first(i, carry):
-        origin = jnp.where(i == 0, me, sibling)
-
-        @pl.when(i == 1)
-        def _():
-            arrived(sibling, 0)
-            arrived(sibling, 1)
-
-        compute(origin)
-        return carry
-
-    lax.fori_loop(0, 2, first, 0)
-
     full = (chips - 1) // 2
+
+    def onward(d, h, kind, act):
+        if (h < PIECES // 2) == (kind == 0):
+            act()
+        else:
+            pl.when(d < full)(act)
 
     def service(d, h):
         for kind, sign, target in ((0, -1, right), (1, 1, left)):
             origin = device_at(place + sign * d, core)
             arrived(origin, h)
-            if h == kind:
-                send(origin, h, kind, target).start()
-            else:
-                @pl.when(d < full)
-                def _():
-                    send(origin, h, kind, target).start()
+            onward(d, h, kind, lambda: send(origin, h, kind, target).start())
             send(origin, h, 2, sibling).start()
 
-    def pair(d, which, wait):
-        def one(i, carry):
-            origin = device_at(place + (2 * i - 1) * d, which)
-            if wait:
-                arrived(origin, 0)
-                arrived(origin, 1)
+    def block_of(d, k):
+        which = core if k < 2 else 1 - core
+        origin = device_at(place + (2 * (k % 2) - 1) * d, which)
+
+        def work():
+            if k >= 2:
+                for h in range(PIECES):
+                    arrived(origin, h)
             compute(origin)
-            return carry
-        lax.fori_loop(0, 2, one, 0)
+
+        if k % 2:
+            pl.when(d > 0)(work)
+        else:
+            work()
 
     def round_of(d, carry):
-        service(d, 0)
-
-        @pl.when(d > 1)
+        for k in range(4):
+            service(d, k)
+            block_of(d - 1, k)
+        return carry
+
+    lax.fori_loop(1, full + 1, round_of, 0)
+    across = device_at(place + length, core)
+
+    def last(k, carry):
+        which = jnp.where(k < 2, core, 1 - core)
+        origin = device_at(place + (2 * (k % 2) - 1) * full, which)
+
+        @pl.when(k >= 2)
         def _():
-            pair(d - 1, 1 - core, True)
-
-        service(d, 1)
-        pair(d, core, False)
+            for h in range(PIECES):
+                arrived(origin, h)
+
+        for h in range(PIECES):
+            @pl.when(k == h)
+            def _():
+                arrived(across, h)
+                send(across, h, 2, sibling).start()
+
+        compute(origin)
         return carry
 
-    lax.fori_loop(1, full + 1, round_of, 0)
-    pair(full, 1 - core, True)
-    across = device_at(place + length, core)
-    for h in range(2):
-        arrived(across, h)
-        send(across, h, 2, sibling).start()
-
-    def last(i, carry):
+    lax.fori_loop(0, 4, last, 0)
+
+    def final(i, carry):
         origin = device_at(place + length, jnp.where(i == 0, core, 1 - core))
 
         @pl.when(i == 1)
         def _():
-            arrived(origin, 0)
-            arrived(origin, 1)
+            for h in range(PIECES):
+                arrived(origin, h)
 
         compute(origin)
         return carry
 
-    lax.fori_loop(0, 2, last, 0)
+    lax.fori_loop(0, 2, final, 0)
 
     app_buf[grp] = -weight * acc[...]
 
@@ -296,18 +301,13 @@
     def sent(d, carry):
         for kind, sign, target in ((0, -1, right), (1, 1, left)):
             origin = device_at(place + sign * d, core)
-            for h in range(2):
-                if h == kind:
-                    send(origin, h, kind, target).wait_send()
-                else:
-                    @pl.when(d < full)
-                    def _():
-                        send(origin, h, kind, target).wait_send()
+            for h in range(PIECES):
+                onward(d, h, kind, lambda: send(origin, h, kind, target).wait_send())
                 send(origin, h, 2, sibling).wait_send()
         return carry
 
     lax.fori_loop(1, full + 1, sent, 0)
-    for h in range(2):
+    for h in range(PIECES):
         send(me, h, 0, right).wait_send()
         send(me, h, 1, left).wait_send()
         send(me, h, 2, sibling).wait_send()
@@ -414,23 +414,22 @@
         rows, norb = orbitals.shape
         weight = 1.0 / (rows * n_blk)
         width = rows // n_grp
-        piece = width // 2
         start = lax.axis_index("grp") * width
-        far_rows = lax.dynamic_slice_in_dim(orbitals, start, width, 0).reshape(2, piece, norb)
+        far_rows = lax.dynamic_slice_in_dim(orbitals, start, width, 0)
         far_coords = lax.dynamic_slice_in_dim(points, start, width, 1)
         far_coords = jnp.pad(far_coords, ((0, PAD - 3), (0, norb - width)))
-        own = jnp.concatenate([far_rows, jnp.broadcast_to(far_coords, (2, PAD, norb))], axis=1)
+        own = jnp.concatenate([far_coords, far_rows], axis=0)
         packed = norb * (norb // BASE + 1) // 2
         share = packed // n_blk
         vmem = pl.BlockSpec(memory_space=pltpu.VMEM)
         dma = pltpu.SemaphoreType.DMA
         applied, corr = pl.pallas_call(
-            functools.partial(apply_kernel, (n_blk, n_grp, inner_two, weight, min(256, rows))),
+            functools.partial(apply_kernel, (n_blk, n_grp, inner_two, weight, min(512, rows))),
             out_shape=[jax.ShapeDtypeStruct((rows, norb), F32), jax.ShapeDtypeStruct((n_blk, share, BASE), F32)],
             in_specs=[vmem] * 3,
             out_specs=[vmem] * 2,
             scratch_shapes=[
-                pltpu.VMEM((n_blk, 2, piece + PAD, norb), F32),
+                pltpu.VMEM((n_blk, PAD + width, norb), F32),
                 pltpu.VMEM((rows, 3 * norb), BF16),
                 pltpu.VMEM((norb, 3 * rows), BF16),
                 pltpu.VMEM((width, 3 * norb), BF16),
@@ -443,7 +442,7 @@
                 pltpu.VMEM((n_grp, share, BASE), F32),
                 pltpu.VMEM((n_blk, share, BASE), F32),
                 pltpu.VMEM((n_grp, rows, norb), F32),
-                dma((n_blk, 2)), dma((3, n_blk, 2)), dma((2,)), dma((chips,)), dma((chips,)),
+                dma((n_blk, PIECES)), dma((3, n_blk, PIECES)), dma((2,)), dma((chips,)), dma((chips,)),
                 dma((n_grp,)), dma((n_grp,)), dma((n_blk,)), dma((chips,)), dma((chips,)),
                 dma((n_grp,)), dma((n_grp,)),
             ],

time: 118 us -> 117 us (level)
  no operation moved by 1% of the time
where the time goes in v3:
time: 117 us
  Pallas kernels  115 us (98%)
  local copies, waits for them, and re-layouts  2.17 us (2%)
    pallas_call x1, Pallas kernels, shards(): pl.pallas_call(functools.partial(apply_kernel, (n_blk, n_grp, inner_two,...  93.9 us
    pallas_call x1, Pallas kernels, shards(): pl.pallas_call(solve_kernel, out_shape=jax.ShapeDtypeStruct((rows, norb),...  21.1 us

profile of v3, /device:TPU:1, one launch (start us, length us, event | category | flops | bytes accessed | tf_op | source)
XLA Modules:
  0.0 117.3 jit_solution(11527032542307573848)
XLA Ops:
  0.0 0.0 copy-start.1
  0.0 0.7 copy-done.1
  0.7 0.1 copy.3
  0.9 0.0 copy-start
  0.9 1.2 constant_dynamic-slice_fusion
  2.1 0.2 copy-done
  2.2 93.9 %apply_and_correlate.1 = (f32[512,512]{1,0:T(8,128)S(1)}, f32[16,80,128]{2,1,0:T(8,128)S(1)}) custom-call(f32[512,512]{1,0:T(8,128)S(1)} %copy-done, f32[264,512]{1,0:T(8,128)S(1)} %select_maximum_fusion.own_ref, f32[512,3]{1,0:T(8,128)S(1)} %bitcast.2), custom_call_target="tpu_custom_call" | custom-call | tf_op jit(solution)/shard_map/apply_and_correlate/pallas_call | solution.py:426
  96.2 21.1 %factor_and_solve.1 = f32[512,512]{1,0:T(8,128)} custom-call(f32[1280,128]{1,0:T(8,128)S(1)} %bitcast.3, f32[512,512]{1,0:T(8,128)S(1)} %get-tuple-element.8.applied_ref), custom_call_target="tpu_custom_call" | custom-call | tf_op jit(solution)/shard_map/factor_and_solve/pallas_call | solution.py:453
  (2 shorter events, 0.0 us)
Async XLA Ops:
  0.0 0.7 copy-start.1
  0.9 1.4 %copy-start = (f32[512,512]{1,0:T(8,128)S(1)}, f32[512,512]{1,0:T(8,128)}, u32[]{:S(2)}) copy-start(f32[512,512]{1,0:T(8,128)} %orb_ref.1) | copy-start | bytes 3145732
